TPU v7x, 32 devices: a whole 2x2x4 slice. The times are simulated.
32 devices in a mesh: parts: 2 (over x), lon: 16 (over z, y, core).
Axes of the slice: x: 2, y: 2, z: 4, core: 2. Of those that a mesh axis runs over, the one named last changes fastest.
Arguments:
- solution: float32 [2048, 32, 512], P(('parts', 'lon')), parts along dimension 0, may hold values from -6 to 6
- residual: float32 [2048, 32, 512], P(('parts', 'lon')), parts along dimension 0, may hold values from -12 to 12
- direction: float32 [2048, 32, 512], P(('parts', 'lon')), parts along dimension 0, may hold values from -12 to 12
- land: int32 [2048, 512], P(('parts', 'lon')), parts along dimension 0, may hold values 0 or 1
- clear: int32 [2048, 32, 512], P(('parts', 'lon')), parts along dimension 0, may hold values 0 or 1
- days: int32 [64], P('parts'), parts along dimension 0, may hold values from 0 to 63, as said below
- mixture: float32 [6, 3, 4], P('parts'), parts along dimension 0, may hold values from 0 to 1024, as said below
- q_lon: bfloat16 [1024, 1024], replicated, may hold values from -0.1875 to 0.1875
- q_lat: bfloat16 [512, 512], replicated, may hold values from -0.25 to 0.25
- q_day: bfloat16 [64, 32], P('parts'), parts along dimension 0, may hold values from -1 to 1
- lam_lon: float32 [1024], replicated, may hold values from 0.2 to 5
- lam_lat: float32 [512], replicated, may hold values from 0.2 to 5
- lam_day: float32 [64], P('parts'), parts along dimension 0, may hold values from 0.2 to 5
- noise: float32 [2], P('parts'), parts along dimension 0, may hold values from 0.5 to 2
- rz_mean: float32 [2], P('parts'), parts along dimension 0, may hold values from 0.25 to 1
Outputs:
- new_solution: float32 [2048, 32, 512], P(('parts', 'lon')), parts along dimension 0
- new_residual: float32 [2048, 32, 512], P(('parts', 'lon')), parts along dimension 0
- new_direction: float32 [2048, 32, 512], P(('parts', 'lon')), parts along dimension 0
- new_rz_mean: float32 [2], P('parts'), parts along dimension 0
There are 2 independent parts, one for each index of `parts`. A program takes and returns all parts, laid end to end along the dimension named above; an argument that names none is the same for every part. Nothing has to cross between parts.
Inputs may be any that keep to these rules, and one draw needn't show every extreme that they name: days[k] is 2 k or 2 k + 1, so the days rise strictly within a record of 64 days; the first is 0 and the last 63. mixture[g, 0] are positive weights, mixture[g, 1] frequencies of at most one half per cell or day, mixture[g, 2] positive length scales in cells or days.
All inputs are finite; a program needn't handle non-finite values. No bound on the sum of `land` or of `clear` on one device may be relied on, other than what follows from the above.
Results may differ from a plain program's by a relative error of at most 0.0018.
Values may be sent and summed in bfloat16 or wider, within the bound.
A program may use at most 128 MiB of HBM per device.

v0:
```python
import functools
import math

import jax
import jax.numpy as jnp
from jax import lax
from jax.experimental import pallas as pl
from jax.experimental.pallas import tpu as pltpu
from jax.sharding import PartitionSpec as P

GROUP = 16
BLOCK = 128
BF = jnp.bfloat16
F32 = jnp.float32


def kernel_values(diff, mix_ref, dim, comps):
    total = jnp.zeros(diff.shape, F32)
    for comp in range(comps):
        weight = mix_ref[dim * 3 * comps + comp]
        freq = mix_ref[dim * 3 * comps + comps + comp]
        length = mix_ref[dim * 3 * comps + 2 * comps + comp]
        ratio = diff / length
        total = total + weight * jnp.exp(-0.5 * ratio * ratio) * jnp.cos(
            2.0 * math.pi * freq * diff
        )
    return total


def fill_toeplitz(out_ref, mix_ref, dim, comps):
    n = out_ref.shape[0]
    diff = (lax.broadcasted_iota(jnp.int32, (1, 2 * n), 1) - n).astype(F32)
    row = kernel_values(diff, mix_ref, dim, comps)
    rolled = pltpu.roll(
        jnp.broadcast_to(row, (BLOCK, 2 * n)), 0, 1, stride=1, stride_axis=0
    )
    for blk in range(n // BLOCK):
        lo = n - BLOCK * blk
        out_ref[BLOCK * blk : BLOCK * (blk + 1), :] = rolled[:, lo : lo + n].astype(BF)


def split(index, low):
    return lax.shift_right_logical(index, low.bit_length() - 1), index & (low - 1)


def block_diagonal(matrix, rows_day_first, cols_day_first):
    n_days = matrix.shape[0]
    size = n_days * GROUP

    def day_lon(index, day_first):
        if day_first:
            return split(index, GROUP)
        lon, day = split(index, n_days)
        return day, lon

    def iota(shape, dim):
        return lax.broadcasted_iota(jnp.int32, shape, dim)

    tall, flat, full = (size, n_days), (n_days, size), (size, size)
    pick_row = day_lon(iota(tall, 0), rows_day_first)[0] == iota(tall, 1)
    pick_col = day_lon(iota(flat, 1), cols_day_first)[0] == iota(flat, 0)
    pick_row = jnp.where(pick_row, 1.0, 0.0).astype(BF)
    pick_col = jnp.where(pick_col, 1.0, 0.0).astype(BF)
    spread = jnp.dot(pick_row, matrix, preferred_element_type=F32).astype(BF)
    spread = jnp.dot(spread, pick_col, preferred_element_type=F32)
    same = day_lon(iota(full, 0), rows_day_first)[1] == day_lon(iota(full, 1), cols_day_first)[1]
    return jnp.where(same, spread, 0.0).astype(BF)


def factor_kernel(
    comps, mix_ref, col_ref, row_ref, q_ref, qt_ref, lat_ref, lon_ref, k_ref, g_ref, h_ref, p_ref
):
    n_days = q_ref.shape[0]
    fill_toeplitz(lat_ref, mix_ref, 1, comps)
    fill_toeplitz(lon_ref, mix_ref, 0, comps)
    k_day = kernel_values(col_ref[...] - row_ref[...], mix_ref, 2, comps).astype(BF)
    k_ref[...] = block_diagonal(k_day, True, False)
    g_ref[...] = block_diagonal(qt_ref[...], True, False)
    h_ref[...] = block_diagonal(q_ref[...], False, True)
    shape = (n_days, n_days)
    eye = lax.broadcasted_iota(jnp.int32, shape, 0) == lax.broadcasted_iota(jnp.int32, shape, 1)
    p_ref[...] = block_diagonal(jnp.where(eye, 1.0, 0.0).astype(BF), False, True)


def factors(n_lon, n_lat, days, mixture, q_day):
    n_days = days.shape[0]
    size = GROUP * n_days
    pos = days.astype(F32)
    vmem = pl.BlockSpec(memory_space=pltpu.VMEM)
    square = jax.ShapeDtypeStruct((size, size), BF)
    return pl.pallas_call(
        functools.partial(factor_kernel, mixture.shape[2]),
        out_shape=[
            jax.ShapeDtypeStruct((n_lat, n_lat), BF),
            jax.ShapeDtypeStruct((n_lon, n_lon), BF),
            square,
            square,
            square,
            square,
        ],
        in_specs=[pl.BlockSpec(memory_space=pltpu.SMEM)] + [vmem] * 4,
        out_specs=[vmem] * 6,
        compiler_params=pltpu.CompilerParams(vmem_limit_bytes=40 * 1024 * 1024),
    )(mixture.reshape(-1), pos[:, None], pos[None, :], q_day, q_day.T)


def dot(left, right):
    return jnp.dot(left, right, preferred_element_type=F32)


def seen(land_ref, clear_ref):
    return (land_ref[...][:, None, :] * clear_ref[...]).astype(F32)


def fold(values):
    wide = jnp.sum(values.reshape(-1, 8, values.shape[-1]), axis=0)
    total = wide[:, 0:128]
    for at in range(128, wide.shape[1], 128):
        total = total + wide[:, at : at + 128]
    return total


def whole_sum(tile_ref):
    return jnp.sum(jnp.sum(tile_ref[...], axis=1, keepdims=True), axis=0, keepdims=True)


def add_tile(sum_ref, tile):
    @pl.when(pl.program_id(0) == 0)
    def _():
        sum_ref[...] = jnp.zeros_like(sum_ref)

    sum_ref[...] += tile


def front(field, day_ref, lat_ref, out_ref):
    a, c, b = field.shape
    one = dot(day_ref[...], field.astype(BF).reshape(a * c, b)).astype(BF)
    out_ref[...] = dot(one, lat_ref[...]).astype(BF).reshape(c, a, b)


def front_kernel(dir_ref, land_ref, clear_ref, day_ref, lat_ref, out_ref):
    front(seen(land_ref, clear_ref) * dir_ref[...], day_ref, lat_ref, out_ref)


def image_kernel(noise_ref, u_ref, dir_ref, land_ref, clear_ref, p_ref, image_ref, sum_ref):
    c, a, b = u_ref.shape
    back = dot(p_ref[...], u_ref[...].reshape(c * a, b)).reshape(a, c, b)
    direction = dir_ref[...]
    image = seen(land_ref, clear_ref) * (back + noise_ref[0] * direction)
    image_ref[...] = image
    add_tile(sum_ref, fold(direction * image))


def update_kernel(
    cells, rz_ref, sum_ref, image_ref, dir_ref, sol_ref, res_ref, land_ref, clear_ref,
    day_ref, lat_ref, new_sol_ref, new_res_ref, out_ref,
):
    alpha = rz_ref[0] * cells / whole_sum(sum_ref)
    alpha = alpha[:, :, None]
    new_sol_ref[...] = sol_ref[...] + alpha * dir_ref[...]
    new_res = res_ref[...] - alpha * image_ref[...]
    new_res_ref[...] = new_res
    front(seen(land_ref, clear_ref) * new_res, day_ref, lat_ref, out_ref)


def precond_kernel(h_ref, res_ref, land_ref, clear_ref, day_ref, lat_ref, out_ref, sum_ref):
    c, a, b = h_ref.shape
    two = lax.dot_general(
        h_ref[...].reshape(c * a, b),
        lat_ref[...],
        (((1,), (1,)), ((), ())),
        preferred_element_type=F32,
    ).astype(BF)
    precond = seen(land_ref, clear_ref) * dot(day_ref[...], two).reshape(a, c, b)
    out_ref[...] = precond
    add_tile(sum_ref, fold(res_ref[...] * precond))


def direction_kernel(cells, rz_ref, sum_ref, pre_ref, dir_ref, out_ref):
    ratio = (whole_sum(sum_ref) / cells) / rz_ref[0]
    out_ref[...] = pre_ref[...] + ratio[:, :, None] * dir_ref[...]


def blocked(kernel, steps, ins, outs):
    specs = {
        "s": lambda shape: pl.BlockSpec(memory_space=pltpu.SMEM),
        "w": lambda shape: pl.BlockSpec(shape, lambda i: (0, 0)),
        "f": lambda shape: pl.BlockSpec((GROUP,) + shape[1:], lambda i: (i, 0, 0)),
        "e": lambda shape: pl.BlockSpec((shape[0], GROUP, shape[2]), lambda i: (0, i, 0)),
        "m": lambda shape: pl.BlockSpec((GROUP, shape[1]), lambda i: (i, 0)),
    }
    return pl.pallas_call(
        kernel,
        grid=(steps,),
        in_specs=[specs[form](array.shape) for form, array in ins],
        out_specs=[specs[form](shape) for form, shape, _ in outs],
        out_shape=[jax.ShapeDtypeStruct(shape, kind) for _, shape, kind in outs],
        compiler_params=pltpu.CompilerParams(vmem_limit_bytes=48 * 1024 * 1024),
    )(*[array for _, array in ins])


def allsum_kernel(n, x_ref, out_ref, buf, send_sem, recv_sem):
    me = lax.axis_index("lon")
    barrier = pltpu.get_barrier_semaphore()

    def greet(p, carry):
        peer = lax.rem(me + p, n)
        pl.semaphore_signal(
            barrier, inc=1, device_id={"lon": peer}, device_id_type=pl.DeviceIdType.MESH
        )
        return carry

    lax.fori_loop(1, n, greet, 0)
    pl.semaphore_wait(barrier, n - 1)

    def copy_to(p):
        return pltpu.make_async_remote_copy(
            src_ref=x_ref,
            dst_ref=buf.at[me],
            send_sem=send_sem.at[p],
            recv_sem=recv_sem.at[p],
            device_id={"lon": lax.rem(me + p, n)},
            device_id_type=pl.DeviceIdType.MESH,
        )

    def start(p, carry):
        copy_to(p).start()
        return carry

    lax.fori_loop(1, n, start, 0)
    buf[pl.ds(me, 1)] = x_ref[...][None]

    def finish(p, carry):
        copy_to(p).wait()
        return carry

    lax.fori_loop(1, n, finish, 0)
    out_ref[...] = jnp.sum(buf[...], axis=0)


def all_sum(tile, n, ident):
    return pl.pallas_call(
        functools.partial(allsum_kernel, n),
        out_shape=jax.ShapeDtypeStruct((8, 128), F32),
        in_specs=[pl.BlockSpec(memory_space=pltpu.VMEM)],
        out_specs=pl.BlockSpec(memory_space=pltpu.VMEM),
        scratch_shapes=[
            pltpu.VMEM((n, 8, 128), F32),
            pltpu.SemaphoreType.DMA((n,)),
            pltpu.SemaphoreType.DMA((n,)),
        ],
        compiler_params=pltpu.CompilerParams(collective_id=ident, has_side_effects=True),
    )(tile)


def lon_kernel(n, scaled, *refs):
    if scaled:
        (x_ref, first_ref, second_ref, left_ref, lat_ref, sigma_ref, y_ref) = refs[:7]
        scratch = refs[7:]
    else:
        x_ref, first_ref, y_ref = refs[:3]
        scratch = refs[3:]
    got, res, mid, send_a, recv_a, send_b, recv_b = scratch
    per, n_lon, width = got.shape
    lon_dev = n_lon // n
    chunk = mid.shape[1]
    halves = width // chunk
    count = per * halves
    rows = min(256, n_lon)
    stride = max(1, n // 2 - 1)
    if math.gcd(stride, n) != 1:
        stride = 1
    me = lax.axis_index("lon")

    barrier = pltpu.get_barrier_semaphore()

    def greet(q, carry):
        pl.semaphore_signal(
            barrier,
            inc=1,
            device_id={"lon": lax.rem(me + q, n)},
            device_id_type=pl.DeviceIdType.MESH,
        )
        return carry

    lax.fori_loop(1, n, greet, 0)
    pl.semaphore_wait(barrier, n - 1)

    def place(k):
        return k // halves, pl.ds(pl.multiple_of((k % halves) * chunk, chunk), chunk)

    def lon_rows(dev):
        return pl.ds(pl.multiple_of(dev * lon_dev, lon_dev), lon_dev)

    def out_copy(k, q):
        r, cols = place(k)
        peer = lax.rem(me + q, n)
        return pltpu.make_async_remote_copy(
            src_ref=x_ref.at[peer * per + r, :, cols],
            dst_ref=got.at[r, lon_rows(me), cols],
            send_sem=send_a.at[k, q],
            recv_sem=recv_a.at[k, q],
            device_id={"lon": peer},
            device_id_type=pl.DeviceIdType.MESH,
        )

    def back_copy(k, q):
        r, cols = place(k)
        peer = lax.rem(me + q, n)
        return pltpu.make_async_remote_copy(
            src_ref=res.at[r, lon_rows(peer), cols],
            dst_ref=y_ref.at[me * per + r, :, cols],
            send_sem=send_b.at[k, q],
            recv_sem=recv_b.at[k, q],
            device_id={"lon": peer},
            device_id_type=pl.DeviceIdType.MESH,
        )

    def over_peers(body):
        def step(t, carry):
            body(lax.rem(t * stride, n))
            return carry

        lax.fori_loop(1, n, step, 0)

    def send_chunk(k, carry):
        over_peers(lambda q: out_copy(k, q).start())
        return carry

    lax.fori_loop(0, count, send_chunk, 0)

    def keep_own(k, carry):
        r, cols = place(k)
        got[r, lon_rows(me), cols] = x_ref[me * per + r, :, cols]
        return carry

    lax.fori_loop(0, count, keep_own, 0)

    def work(k, carry):
        r, cols = place(k)
        over_peers(lambda q: out_copy(k, q).wait_recv())

        def first(i, inner):
            at = pl.ds(pl.multiple_of(i * rows, rows), rows)
            prod = jnp.dot(first_ref[at, :], got[r, :, cols], preferred_element_type=F32)
            if scaled:
                g_three = prod.astype(BF).astype(F32)
                denom = left_ref[r, at, :] * lat_ref[:, cols] + sigma_ref[...]
                mid[at, :] = (g_three / denom).astype(BF)
            else:
                res[r, at, cols] = prod.astype(BF)
            return inner

        lax.fori_loop(0, n_lon // rows, first, 0)
        if scaled:

            def second(i, inner):
                at = pl.ds(pl.multiple_of(i * rows, rows), rows)
                res[r, at, cols] = jnp.dot(
                    second_ref[at, :], mid[...], preferred_element_type=F32
                ).astype(BF)
                return inner

            lax.fori_loop(0, n_lon // rows, second, 0)
        over_peers(lambda q: back_copy(k, q).start())
        y_ref[me * per + r, :, cols] = res[r, lon_rows(me), cols]
        return carry

    lax.fori_loop(0, count, work, 0)

    def finish(k, carry):
        over_peers(lambda q: out_copy(k, q).wait_send())
        over_peers(lambda q: back_copy(k, q).wait())
        return carry

    lax.fori_loop(0, count, finish, 0)


def lon_products(field, n, pieces, factors, scales, ident):
    c, a, b = field.shape
    n_lon = a * n
    if pieces > 1:
        field = field.reshape(c, a, pieces, b // pieces).transpose(0, 2, 1, 3)
        field = field.reshape(c * pieces, a, b // pieces)
    per = field.shape[0] // n
    width = field.shape[2]
    chunk = min(256, width)
    count = per * (width // chunk)
    vmem = pl.BlockSpec(memory_space=pltpu.VMEM)
    flops = 2 * len(factors) * n_lon * n_lon * per * width
    out = pl.pallas_call(
        functools.partial(lon_kernel, n, bool(scales)),
        out_shape=jax.ShapeDtypeStruct(field.shape, BF),
        in_specs=[vmem] * (1 + len(factors) + len(scales)),
        out_specs=vmem,
        scratch_shapes=[
            pltpu.VMEM((per, n_lon, width), BF),
            pltpu.VMEM((per, n_lon, width), BF),
            pltpu.VMEM((n_lon, chunk), BF),
            pltpu.SemaphoreType.DMA((count, n)),
            pltpu.SemaphoreType.DMA((count, n)),
            pltpu.SemaphoreType.DMA((count, n)),
            pltpu.SemaphoreType.DMA((count, n)),
        ],
        compiler_params=pltpu.CompilerParams(
            collective_id=ident, has_side_effects=True, vmem_limit_bytes=40 * 1024 * 1024
        ),
        cost_estimate=pl.CostEstimate(
            flops=flops, bytes_accessed=4 * field.size, transcendentals=0
        ),
    )(field, *factors, *scales)
    if pieces > 1:
        out = out.reshape(c, pieces, a, b // pieces).transpose(0, 2, 1, 3)
        out = out.reshape(c, a, b)
    return out


def day_major(matrix):
    n_days = matrix.shape[0]
    eye = jnp.eye(GROUP, dtype=BF)
    full = matrix[:, None, None, :] * eye[None, :, :, None]
    return full.reshape(GROUP * n_days, GROUP * n_days)


def lon_major(matrix):
    n_days = matrix.shape[0]
    eye = jnp.eye(GROUP, dtype=BF)
    full = matrix[None, :, :, None] * eye[:, None, None, :]
    return full.reshape(GROUP * n_days, GROUP * n_days)


def mm(spec, left, right):
    return jnp.einsum(spec, left, right, preferred_element_type=F32)


def on_device(
    n,
    solution,
    residual,
    direction,
    land,
    clear,
    days,
    mixture,
    q_lon,
    q_lat,
    q_day,
    lam_lon,
    lam_lat,
    lam_day,
    noise,
    rz_mean,
):
    shape = solution.shape
    lon_dev, n_days, n_lat = shape
    n_lon = q_lon.shape[0]
    cells = n_lon * n_days * n_lat
    pieces = max(1, n // n_days)
    steps = lon_dev // GROUP
    by_day = (n_days, lon_dev, n_lat)
    tile = ("w", (8, 128), F32)
    k_lat, k_lon, k_mix, g_mix, h_mix, permute = factors(n_lon, n_lat, days, mixture, q_day)

    masks = [("m", land), ("f", clear)]
    (third,) = blocked(
        front_kernel,
        steps,
        [("f", direction), *masks, ("w", k_mix), ("w", k_lat)],
        [("e", by_day, BF)],
    )
    fourth = lon_products(third, n, pieces, (k_lon,), (), 2)
    image, partial = blocked(
        image_kernel,
        steps,
        [("s", noise), ("e", fourth), ("f", direction), *masks, ("w", permute)],
        [("f", shape, F32), tile],
    )
    curvature = all_sum(partial, n, 1)
    new_solution, new_residual, g_two = blocked(
        functools.partial(update_kernel, float(cells)),
        steps,
        [
            ("s", rz_mean),
            ("w", curvature),
            ("f", image),
            ("f", direction),
            ("f", solution),
            ("f", residual),
            *masks,
            ("w", g_mix),
            ("w", q_lat),
        ],
        [("f", shape, F32), ("f", shape, F32), ("e", by_day, BF)],
    )

    per = n_days * pieces // n
    width = n_lat // pieces
    at = lax.axis_index("lon")
    day_own = lax.dynamic_slice_in_dim(lam_day, at * per // pieces, per)
    lat_own = lax.dynamic_slice_in_dim(lam_lat, (at % pieces) * width, width)
    left = lam_lon[None, :, None] * day_own[:, None, None]
    scales = (left, lat_own[None, :], noise.reshape(1, 1))
    h_local = lon_products(g_two, n, pieces, (q_lon.T, q_lon), scales, 3)
    precond, partial = blocked(
        precond_kernel,
        steps,
        [("e", h_local), ("f", new_residual), *masks, ("w", h_mix), ("w", q_lat)],
        [("f", shape, F32), tile],
    )
    total = all_sum(partial, n, 1)
    (new_direction,) = blocked(
        functools.partial(direction_kernel, float(cells)),
        steps,
        [("s", rz_mean), ("w", total), ("f", precond), ("f", direction)],
        [("f", shape, F32)],
    )
    new_rz = jnp.sum(total) / cells
    return (new_solution, new_residual, new_direction, new_rz.reshape(1))


def solution(mesh):
    in_specs = (
        P(("parts", "lon"), None, None),
        P(("parts", "lon"), None, None),
        P(("parts", "lon"), None, None),
        P(("parts", "lon"), None),
        P(("parts", "lon"), None, None),
        P("parts"),
        P("parts", None, None),
        P(),
        P(),
        P("parts", None),
        P(),
        P(),
        P("parts"),
        P("parts"),
        P("parts"),
    )
    out_specs = (
        P(("parts", "lon"), None, None),
        P(("parts", "lon"), None, None),
        P(("parts", "lon"), None, None),
        P("parts"),
    )
    return jax.shard_map(
        functools.partial(on_device, mesh.shape["lon"]),
        mesh=mesh,
        in_specs=in_specs,
        out_specs=out_specs,
        check_vma=False,
    )
```

profile of v0, /device:TPU:0, one launch (start us, length us, event | category | flops | bytes accessed | tf_op | source)
XLA Modules:
  0.0 273.8 jit_solution(12678514332489047770)
XLA Ops:
  1.9 0.8 reshape.65.mix_ref
  2.7 0.7 convert_bitcast_fusion
  3.4 0.1 copy.20.col_ref
  3.5 0.8 copy.19
  4.2 0.0 copy-start.10
  4.2 0.7 copy-done.10
  4.9 3.5 %shard_map.174 = (bf16[512,512]{1,0:T(8,128)(2,1)S(1)}, bf16[1024,1024]{1,0:T(8,128)(2,1)S(1)}, bf16[512,512]{1,0:T(8,128)(2,1)S(1)}, bf16[512,512]{1,0:T(8,128)...) custom-call(f32[36]{0:T(128)S(1)} %reshape.65.mix_ref, f32[32,1]{1,0:T(8,128)S(1)} %copy.20.col_ref, ...), custom_call_target="tpu_custom_call" | custom-call | tf_op jit(solution)/shard_map/pallas_call | solution.py:91
  8.4 0.0 copy-start.6
  8.4 0.8 copy-done.6
  9.2 0.0 copy-start.1
  9.2 0.9 copy-done.1
  10.1 5.6 %shard_map.175.refs_0_ = bf16[32,64,512]{2,1,0:T(8,128)(2,1)S(1)} custom-call(f32[64,32,512]{2,1,0:T(8,128)} %dir_ref.7, s32[64,512]{1,0:T(8,128)S(1)} %copy-done.1, s32[64,32,512]{2,1,0:T(8,128)} %clear_ref.7, bf16[512,512]{1,0:T(8,128)(2,1)S(1)} %get-tuple-element.17.day_ref, bf16[512,512]{1,0:T(8,128)(2,1)S(1)} %get-tuple-element.18.lat_ref), custom_call_target="tpu_custom_call" | custom-call | tf_op jit(solution)/shard_map/pallas_call | solution.py:192
  15.7 0.0 copy-start.2
  15.7 97.9 %shard_map.176.u_ref = bf16[32,64,512]{2,1,0:T(8,128)(2,1)S(1)} custom-call(bf16[32,64,512]{2,1,0:T(8,128)(2,1)S(1)} %shard_map.175.refs_0_, bf16[1024,1024]{1,0:T(8,128)(2,1)S(1)} %get-tuple-element.19.refs_1_), custom_call_target="tpu_custom_call" | custom-call | flops 2147483648 | bytes 4194304 | tf_op jit(solution)/shard_map/pallas_call | solution.py:391
  113.7 0.0 copy-done.2
  113.7 0.0 copy-start.5
  113.7 6.7 %shard_map.177 = (f32[64,32,512]{2,1,0:T(8,128)}, f32[8,128]{1,0:T(8,128)S(1)}) custom-call(f32[1]{0:T(128)} %copy.22.noise_ref, bf16[32,64,512]{2,1,0:T(8,128)(2,1)S(1)} %shard_map.176.u_ref, f32[64,32,512]{2,1,0:T(8,128)} %dir_ref.7, s32[64,512]{1,0:T(8,128)S(1)} %copy-done.2, s32[64,32,512]{2,1,0:T(8,128)} %clear_ref.7, ...), custom_call_target="tpu_custom_call" | custom-call | tf_op jit(solution)/shard_map/pallas_call | solution.py:192
  120.4 0.0 copy-start.12
  120.4 0.6 copy-done.12
  121.0 9.8 %shard_map.178.sum_ref = f32[8,128]{1,0:T(8,128)} custom-call(f32[8,128]{1,0:T(8,128)} %copy-done.12), custom_call_target="tpu_custom_call" | custom-call | tf_op jit(solution)/shard_map/pallas_call | solution.py:242
  130.8 0.0 copy-done.5
  130.8 0.0 copy-start.7
  130.8 1.0 copy-done.7
  131.9 0.0 copy-start.11
  131.9 0.7 copy-done.11
  132.5 0.0 copy-start.3
  132.5 10.8 %shard_map.179 = (f32[64,32,512]{2,1,0:T(8,128)}, f32[64,32,512]{2,1,0:T(8,128)}, bf16[32,64,512]{2,1,0:T(8,128)(2,1)S(1)}) custom-call(f32[1]{0:T(128)S(6)} %copy.23.rz_ref, f32[8,128]{1,0:T(8,128)S(1)} %copy-done.11, f32[64,32,512]{2,1,0:T(8,128)} %get-tuple-element.22.image_ref, f32[64,32,512]{2,1,0:T(8,128)} %dir_ref.7, f32[64,32,512]{2,1,0:T(8,128)} %sol_ref.1, ...), custom_call_target="tpu_custom_call" | custom-call | tf_op jit(solution)/shard_map/pallas_call | solution.py:192
  143.3 0.0 copy-start.14
  143.3 1.3 copy-done.14
  144.6 0.0 copy-start.18
  144.6 0.0 copy-start.17
  144.6 0.0 copy-start.16
  144.6 0.0 copy-done.3
  144.6 2.6 copy.21
  147.2 0.0 copy-done.18
  147.2 0.1 dynamic_slice.4
  147.3 0.0 copy-done.17
  147.3 0.2 broadcast_multiply_fusion.refs_3_
  147.5 0.0 copy-done.16
  147.5 0.0 copy-start.4
  147.5 1.6 copy-done.4
  149.1 0.0 copy-start.15
  149.1 1.6 copy-done.15
  150.7 95.6 %shard_map.180.h_ref = bf16[32,64,512]{2,1,0:T(8,128)(2,1)S(1)} custom-call(bf16[32,64,512]{2,1,0:T(8,128)(2,1)S(1)} %copy-done.15, bf16[1024,1024]{1,0:T(8,128)(2,1)S(1)} %bitcast.10, bf16[1024,1024]{1,0:T(8,128)(2,1)S(1)} %copy-done.3, f32[2,1024,1]{2,1,0:T(8,128)S(1)} %broadcast_multiply_fusion.refs_3_, f32[1,512]{1,0:T(1,128)S(1)} %bitcast.12, ...), custom_call_target="tpu_custom_call" | custom-call | flops 4294967296 | bytes 4194304 | tf_op jit(solution)/shard_map/pallas_call | solution.py:391
  246.3 7.3 %shard_map.181 = (f32[64,32,512]{2,1,0:T(8,128)}, f32[8,128]{1,0:T(8,128)S(1)}) custom-call(bf16[32,64,512]{2,1,0:T(8,128)(2,1)S(1)} %shard_map.180.h_ref, f32[64,32,512]{2,1,0:T(8,128)} %get-tuple-element.14.res_ref, s32[64,512]{1,0:T(8,128)S(1)} %copy-done.2, s32[64,32,512]{2,1,0:T(8,128)} %clear_ref.7, bf16[512,512]{1,0:T(8,128)(2,1)S(1)} %get-tuple-element.27.day_ref, ...), custom_call_target="tpu_custom_call" | custom-call | tf_op jit(solution)/shard_map/pallas_call | solution.py:192
  253.7 0.0 copy-start.13
  253.7 0.6 copy-done.13
  254.3 9.2 %shard_map.182.sum_ref = f32[8,128]{1,0:T(8,128)} custom-call(f32[8,128]{1,0:T(8,128)} %copy-done.13), custom_call_target="tpu_custom_call" | custom-call | tf_op jit(solution)/shard_map/pallas_call | solution.py:242
  263.5 0.0 copy-start
  263.5 2.2 copy-done
  265.7 0.0 copy-start.8
  265.7 0.7 copy-done.8
  266.4 0.0 copy-start.9
  266.4 5.0 %shard_map.183 = f32[64,32,512]{2,1,0:T(8,128)} custom-call(f32[1]{0:T(128)S(6)} %copy.23.rz_ref, f32[8,128]{1,0:T(8,128)S(1)} %copy-done.8, f32[64,32,512]{2,1,0:T(8,128)S(1)} %copy-done, f32[64,32,512]{2,1,0:T(8,128)} %dir_ref.7), custom_call_target="tpu_custom_call" | custom-call | tf_op jit(solution)/shard_map/pallas_call | solution.py:192
  271.4 0.0 copy-done.9
  271.4 0.6 reduce_sum.9
Async XLA Ops:
  4.2 0.7 copy-start.10
  8.4 0.8 copy-start.6
  9.2 0.9 copy-start.1
  15.7 97.9 %copy-start.2 = (s32[64,512]{1,0:T(8,128)S(1)}, s32[64,512]{1,0:T(8,128)}, u32[]{:S(2)}) copy-start(s32[64,512]{1,0:T(8,128)} %land_ref.7) | copy-start | bytes 393220
  113.7 17.1 %copy-start.5 = (bf16[512,512]{1,0:T(8,128)(2,1)S(1)}, bf16[512,512]{1,0:T(8,128)(2,1)}, u32[]{:S(2)}) copy-start(bf16[512,512]{1,0:T(8,128)(2,1)} %lat_ref.3) | copy-start | bytes 1572868
  120.4 0.6 copy-start.12
  130.8 1.0 copy-start.7
  131.9 0.7 copy-start.11
  132.5 12.1 %copy-start.3 = (bf16[1024,1024]{1,0:T(8,128)(2,1)S(1)}, bf16[1024,1024]{1,0:T(8,128)(2,1)}, u32[]{:S(2)}) copy-start(bf16[1024,1024]{1,0:T(8,128)(2,1)} %refs_2_.1) | copy-start | bytes 6291460
  143.3 1.3 copy-start.14
  144.6 2.6 copy-start.18
  144.6 2.7 copy-start.17
  144.6 2.9 %copy-start.16 = (f32[512]{0:T(512)S(1)}, f32[512]{0:T(512)}, u32[]{:S(2)}) copy-start(f32[512]{0:T(512)} %param.26) | copy-start | bytes 6148
  147.5 1.6 copy-start.4
  149.1 1.6 copy-start.15
  253.7 0.6 copy-start.13
  263.5 2.2 copy-start
  265.7 0.7 copy-start.8
  266.4 5.0 %copy-start.9 = (f32[8,128]{1,0:T(8,128)S(1)}, f32[8,128]{1,0:T(8,128)}, u32[]{:S(2)}) copy-start(f32[8,128]{1,0:T(8,128)} %shard_map.182.sum_ref) | copy-start | bytes 12292
where the time goes:
time: 275 us; the launch traced here: 274 us
  Pallas kernels  251 us (91%)
  local copies, waits for them, and re-layouts  17 us (6%)
  between operations  3.85 us (1%)
    pallas_call x2, Pallas kernels, lon_products(): pl.pallas_call(functools.partial(lon_kernel, n, bool(scales)), out_shape=...  194 us
    pallas_call x5, Pallas kernels, blocked(): pl.pallas_call(kernel, grid=(steps,), in_specs=[specs[form](array.shape)...  35.4 us
    pallas_call x2, Pallas kernels, all_sum(): pl.pallas_call(functools.partial(allsum_kernel, n), out_shape=jax.ShapeDt...  19.1 us
    unnamed x40, local copies, waits for them, and re-layouts  16 us

commit v1 on v0

--- a/solution.py
+++ b/solution.py
@@ -124,12 +124,64 @@
     return jnp.sum(jnp.sum(tile_ref[...], axis=1, keepdims=True), axis=0, keepdims=True)
 
 
-def add_tile(sum_ref, tile):
+def greet_peers(n):
+    me = lax.axis_index("lon")
+    barrier = pltpu.get_barrier_semaphore()
+
+    def greet(q, carry):
+        pl.semaphore_signal(
+            barrier,
+            inc=1,
+            device_id={"lon": lax.rem(me + q, n)},
+            device_id_type=pl.DeviceIdType.MESH,
+        )
+        return carry
+
+    lax.fori_loop(1, n, greet, 0)
+
+
+def greet_first(n):
     @pl.when(pl.program_id(0) == 0)
     def _():
-        sum_ref[...] = jnp.zeros_like(sum_ref)
-
-    sum_ref[...] += tile
+        greet_peers(n)
+
+
+def sum_tiles(n, tile, sum_ref, own, buf, send_sem, recv_sem):
+    step = pl.program_id(0)
+
+    @pl.when(step == 0)
+    def _():
+        own[...] = jnp.zeros_like(own)
+
+    own[...] += tile
+
+    @pl.when(step == pl.num_programs(0) - 1)
+    def _():
+        me = lax.axis_index("lon")
+        pl.semaphore_wait(pltpu.get_barrier_semaphore(), n - 1)
+
+        def copy_to(q):
+            return pltpu.make_async_remote_copy(
+                src_ref=own,
+                dst_ref=buf.at[me],
+                send_sem=send_sem.at[q],
+                recv_sem=recv_sem.at[q],
+                device_id={"lon": lax.rem(me + q, n)},
+                device_id_type=pl.DeviceIdType.MESH,
+            )
+
+        def start(q, carry):
+            copy_to(q).start()
+            return carry
+
+        def finish(q, carry):
+            copy_to(q).wait()
+            return carry
+
+        lax.fori_loop(1, n, start, 0)
+        buf[pl.ds(me, 1)] = own[...][None]
+        lax.fori_loop(1, n, finish, 0)
+        sum_ref[...] = jnp.sum(buf[...], axis=0)
 
 
 def front(field, day_ref, lat_ref, out_ref):
@@ -142,13 +194,16 @@
     front(seen(land_ref, clear_ref) * dir_ref[...], day_ref, lat_ref, out_ref)
 
 
-def image_kernel(noise_ref, u_ref, dir_ref, land_ref, clear_ref, p_ref, image_ref, sum_ref):
+def image_kernel(
+    n, noise_ref, u_ref, dir_ref, land_ref, clear_ref, p_ref, image_ref, sum_ref, *scratch
+):
+    greet_first(n)
     c, a, b = u_ref.shape
     back = dot(p_ref[...], u_ref[...].reshape(c * a, b)).reshape(a, c, b)
     direction = dir_ref[...]
     image = seen(land_ref, clear_ref) * (back + noise_ref[0] * direction)
     image_ref[...] = image
-    add_tile(sum_ref, fold(direction * image))
+    sum_tiles(n, fold(direction * image), sum_ref, *scratch)
 
 
 def update_kernel(
@@ -163,7 +218,10 @@
     front(seen(land_ref, clear_ref) * new_res, day_ref, lat_ref, out_ref)
 
 
-def precond_kernel(h_ref, res_ref, land_ref, clear_ref, day_ref, lat_ref, out_ref, sum_ref):
+def precond_kernel(
+    n, h_ref, res_ref, land_ref, clear_ref, day_ref, lat_ref, out_ref, sum_ref, *scratch
+):
+    greet_first(n)
     c, a, b = h_ref.shape
     two = lax.dot_general(
         h_ref[...].reshape(c * a, b),
@@ -173,7 +231,7 @@
     ).astype(BF)
     precond = seen(land_ref, clear_ref) * dot(day_ref[...], two).reshape(a, c, b)
     out_ref[...] = precond
-    add_tile(sum_ref, fold(res_ref[...] * precond))
+    sum_tiles(n, fold(res_ref[...] * precond), sum_ref, *scratch)
 
 
 def direction_kernel(cells, rz_ref, sum_ref, pre_ref, dir_ref, out_ref):
@@ -181,7 +239,7 @@
     out_ref[...] = pre_ref[...] + ratio[:, :, None] * dir_ref[...]
 
 
-def blocked(kernel, steps, ins, outs):
+def blocked(kernel, steps, ins, outs, n=0, ident=None):
     specs = {
         "s": lambda shape: pl.BlockSpec(memory_space=pltpu.SMEM),
         "w": lambda shape: pl.BlockSpec(shape, lambda i: (0, 0)),
@@ -189,74 +247,31 @@
         "e": lambda shape: pl.BlockSpec((shape[0], GROUP, shape[2]), lambda i: (0, i, 0)),
         "m": lambda shape: pl.BlockSpec((GROUP, shape[1]), lambda i: (i, 0)),
     }
+    scratch, remote = [], {}
+    if ident is not None:
+        scratch = [
+            pltpu.VMEM((8, 128), F32),
+            pltpu.VMEM((n, 8, 128), F32),
+            pltpu.SemaphoreType.DMA((n,)),
+            pltpu.SemaphoreType.DMA((n,)),
+        ]
+        remote = dict(collective_id=ident, has_side_effects=True)
     return pl.pallas_call(
         kernel,
         grid=(steps,),
+        scratch_shapes=scratch,
         in_specs=[specs[form](array.shape) for form, array in ins],
         out_specs=[specs[form](shape) for form, shape, _ in outs],
         out_shape=[jax.ShapeDtypeStruct(shape, kind) for _, shape, kind in outs],
-        compiler_params=pltpu.CompilerParams(vmem_limit_bytes=48 * 1024 * 1024),
+        compiler_params=pltpu.CompilerParams(vmem_limit_bytes=48 * 1024 * 1024, **remote),
     )(*[array for _, array in ins])
-
-
-def allsum_kernel(n, x_ref, out_ref, buf, send_sem, recv_sem):
-    me = lax.axis_index("lon")
-    barrier = pltpu.get_barrier_semaphore()
-
-    def greet(p, carry):
-        peer = lax.rem(me + p, n)
-        pl.semaphore_signal(
-            barrier, inc=1, device_id={"lon": peer}, device_id_type=pl.DeviceIdType.MESH
-        )
-        return carry
-
-    lax.fori_loop(1, n, greet, 0)
-    pl.semaphore_wait(barrier, n - 1)
-
-    def copy_to(p):
-        return pltpu.make_async_remote_copy(
-            src_ref=x_ref,
-            dst_ref=buf.at[me],
-            send_sem=send_sem.at[p],
-            recv_sem=recv_sem.at[p],
-            device_id={"lon": lax.rem(me + p, n)},
-            device_id_type=pl.DeviceIdType.MESH,
-        )
-
-    def start(p, carry):
-        copy_to(p).start()
-        return carry
-
-    lax.fori_loop(1, n, start, 0)
-    buf[pl.ds(me, 1)] = x_ref[...][None]
-
-    def finish(p, carry):
-        copy_to(p).wait()
-        return carry
-
-    lax.fori_loop(1, n, finish, 0)
-    out_ref[...] = jnp.sum(buf[...], axis=0)
-
-
-def all_sum(tile, n, ident):
-    return pl.pallas_call(
-        functools.partial(allsum_kernel, n),
-        out_shape=jax.ShapeDtypeStruct((8, 128), F32),
-        in_specs=[pl.BlockSpec(memory_space=pltpu.VMEM)],
-        out_specs=pl.BlockSpec(memory_space=pltpu.VMEM),
-        scratch_shapes=[
-            pltpu.VMEM((n, 8, 128), F32),
-            pltpu.SemaphoreType.DMA((n,)),
-            pltpu.SemaphoreType.DMA((n,)),
-        ],
-        compiler_params=pltpu.CompilerParams(collective_id=ident, has_side_effects=True),
-    )(tile)
 
 
 def lon_kernel(n, scaled, *refs):
     if scaled:
-        (x_ref, first_ref, second_ref, left_ref, lat_ref, sigma_ref, y_ref) = refs[:7]
-        scratch = refs[7:]
+        x_ref, second_ref, left_ref, lat_ref, sigma_ref, y_ref = refs[:6]
+        first_ref = refs[-1]
+        scratch = refs[6:-1]
     else:
         x_ref, first_ref, y_ref = refs[:3]
         scratch = refs[3:]
@@ -272,19 +287,8 @@
         stride = 1
     me = lax.axis_index("lon")
 
-    barrier = pltpu.get_barrier_semaphore()
-
-    def greet(q, carry):
-        pl.semaphore_signal(
-            barrier,
-            inc=1,
-            device_id={"lon": lax.rem(me + q, n)},
-            device_id_type=pl.DeviceIdType.MESH,
-        )
-        return carry
-
-    lax.fori_loop(1, n, greet, 0)
-    pl.semaphore_wait(barrier, n - 1)
+    greet_peers(n)
+    pl.semaphore_wait(pltpu.get_barrier_semaphore(), n - 1)
 
     def place(k):
         return k // halves, pl.ds(pl.multiple_of((k % halves) * chunk, chunk), chunk)
@@ -335,6 +339,14 @@
         return carry
 
     lax.fori_loop(0, count, keep_own, 0)
+    if scaled:
+
+        def turn(i, carry):
+            at = pl.ds(pl.multiple_of(i * rows, rows), rows)
+            first_ref[at, :] = second_ref[:, at].T
+            return carry
+
+        lax.fori_loop(0, n_lon // rows, turn, 0)
 
     def work(k, carry):
         r, cols = place(k)
@@ -376,7 +388,7 @@
     lax.fori_loop(0, count, finish, 0)
 
 
-def lon_products(field, n, pieces, factors, scales, ident):
+def lon_products(field, n, pieces, factor, scales, ident):
     c, a, b = field.shape
     n_lon = a * n
     if pieces > 1:
@@ -387,11 +399,11 @@
     chunk = min(256, width)
     count = per * (width // chunk)
     vmem = pl.BlockSpec(memory_space=pltpu.VMEM)
-    flops = 2 * len(factors) * n_lon * n_lon * per * width
+    flops = 2 * (2 if scales else 1) * n_lon * n_lon * per * width
     out = pl.pallas_call(
         functools.partial(lon_kernel, n, bool(scales)),
         out_shape=jax.ShapeDtypeStruct(field.shape, BF),
-        in_specs=[vmem] * (1 + len(factors) + len(scales)),
+        in_specs=[vmem] * (2 + len(scales)),
         out_specs=vmem,
         scratch_shapes=[
             pltpu.VMEM((per, n_lon, width), BF),
@@ -401,14 +413,15 @@
             pltpu.SemaphoreType.DMA((count, n)),
             pltpu.SemaphoreType.DMA((count, n)),
             pltpu.SemaphoreType.DMA((count, n)),
-        ],
+        ]
+        + ([pltpu.VMEM((n_lon, n_lon), BF)] if scales else []),
         compiler_params=pltpu.CompilerParams(
             collective_id=ident, has_side_effects=True, vmem_limit_bytes=40 * 1024 * 1024
         ),
         cost_estimate=pl.CostEstimate(
             flops=flops, bytes_accessed=4 * field.size, transcendentals=0
         ),
-    )(field, *factors, *scales)
+    )(field, factor, *scales)
     if pieces > 1:
         out = out.reshape(c, pieces, a, b // pieces).transpose(0, 2, 1, 3)
         out = out.reshape(c, a, b)
@@ -468,14 +481,15 @@
         [("f", direction), *masks, ("w", k_mix), ("w", k_lat)],
         [("e", by_day, BF)],
     )
-    fourth = lon_products(third, n, pieces, (k_lon,), (), 2)
-    image, partial = blocked(
-        image_kernel,
+    fourth = lon_products(third, n, pieces, k_lon, (), 2)
+    image, curvature = blocked(
+        functools.partial(image_kernel, n),
         steps,
         [("s", noise), ("e", fourth), ("f", direction), *masks, ("w", permute)],
         [("f", shape, F32), tile],
-    )
-    curvature = all_sum(partial, n, 1)
+        n,
+        1,
+    )
     new_solution, new_residual, g_two = blocked(
         functools.partial(update_kernel, float(cells)),
         steps,
@@ -500,14 +514,15 @@
     lat_own = lax.dynamic_slice_in_dim(lam_lat, (at % pieces) * width, width)
     left = lam_lon[None, :, None] * day_own[:, None, None]
     scales = (left, lat_own[None, :], noise.reshape(1, 1))
-    h_local = lon_products(g_two, n, pieces, (q_lon.T, q_lon), scales, 3)
-    precond, partial = blocked(
-        precond_kernel,
+    h_local = lon_products(g_two, n, pieces, q_lon, scales, 3)
+    precond, total = blocked(
+        functools.partial(precond_kernel, n),
         steps,
         [("e", h_local), ("f", new_residual), *masks, ("w", h_mix), ("w", q_lat)],
         [("f", shape, F32), tile],
-    )
-    total = all_sum(partial, n, 1)
+        n,
+        4,
+    )
     (new_direction,) = blocked(
         functools.partial(direction_kernel, float(cells)),
         steps,

time: 275 us -> 259 us (0.942)
  local copies, waits for them, and re-layouts: 17 us -> 8.44 us
  Pallas kernels: 251 us -> 245 us
    unnamed x40 -> x23, local copies, waits for them, and re-layouts: 16 us -> 7.5 us
    pallas_call x7 -> x5, Pallas kernels: 54.5 us -> 48 us  [blocked(): pl.pallas_call(kernel, grid=(steps,), scratch_shapes=scratch, in_specs=[s...]
where the time goes in v1:
time: 259 us
  Pallas kernels  245 us (95%)
  local copies, waits for them, and re-layouts  8.44 us (3%)
  between operations  3.87 us (1%)
    pallas_call x2, Pallas kernels, lon_products(): pl.pallas_call(functools.partial(lon_kernel, n, bool(scales)), out_shape=...  193 us
    pallas_call x5, Pallas kernels, blocked(): pl.pallas_call(kernel, grid=(steps,), scratch_shapes=scratch, in_specs=[s...  48 us
    unnamed x23, local copies, waits for them, and re-layouts  7.5 us

profile of v1, /device:TPU:0, one launch (start us, length us, event | category | flops | bytes accessed | tf_op | source)
XLA Modules:
  0.0 258.6 jit_solution(2217807803354128617)
XLA Ops:
  1.9 0.8 reshape.65.mix_ref
  2.7 0.7 convert_bitcast_fusion
  3.4 0.1 copy.20.col_ref
  3.5 0.8 copy.19
  4.2 0.0 copy-start.4
  4.2 0.7 copy-done.4
  4.9 3.5 %shard_map.174 = (bf16[512,512]{1,0:T(8,128)(2,1)S(1)}, bf16[1024,1024]{1,0:T(8,128)(2,1)S(1)}, bf16[512,512]{1,0:T(8,128)(2,1)S(1)}, bf16[512,512]{1,0:T(8,128)...) custom-call(f32[36]{0:T(128)S(1)} %reshape.65.mix_ref, f32[32,1]{1,0:T(8,128)S(1)} %copy.20.col_ref, ...), custom_call_target="tpu_custom_call" | custom-call | tf_op jit(solution)/shard_map/pallas_call | solution.py:91
  8.4 0.0 copy-start.1
  8.4 0.9 copy-done.1
  9.3 5.6 %shard_map.175.refs_0_ = bf16[32,64,512]{2,1,0:T(8,128)(2,1)S(1)} custom-call(f32[64,32,512]{2,1,0:T(8,128)} %dir_ref.7, s32[64,512]{1,0:T(8,128)S(1)} %copy-done.1, s32[64,32,512]{2,1,0:T(8,128)} %clear_ref.7, bf16[512,512]{1,0:T(8,128)(2,1)S(1)} %get-tuple-element.17.day_ref, bf16[512,512]{1,0:T(8,128)(2,1)S(1)} %get-tuple-element.18.lat_ref), custom_call_target="tpu_custom_call" | custom-call | tf_op jit(solution)/shard_map/pallas_call | solution.py:259
  14.9 0.0 copy-start.2
  14.9 97.9 %shard_map.176.u_ref = bf16[32,64,512]{2,1,0:T(8,128)(2,1)S(1)} custom-call(bf16[32,64,512]{2,1,0:T(8,128)(2,1)S(1)} %shard_map.175.refs_0_, bf16[1024,1024]{1,0:T(8,128)(2,1)S(1)} %get-tuple-element.19.refs_1_), custom_call_target="tpu_custom_call" | custom-call | flops 2147483648 | bytes 4194304 | tf_op jit(solution)/shard_map/pallas_call | solution.py:403
  112.9 0.0 copy-done.2
  112.9 0.0 copy-start.3
  112.9 13.7 %shard_map.177 = (f32[64,32,512]{2,1,0:T(8,128)}, f32[8,128]{1,0:T(8,128)S(1)}) custom-call(f32[1]{0:T(128)} %copy.21.noise_ref, bf16[32,64,512]{2,1,0:T(8,128)(2,1)S(1)} %shard_map.176.u_ref, f32[64,32,512]{2,1,0:T(8,128)} %dir_ref.7, s32[64,512]{1,0:T(8,128)S(1)} %copy-done.2, s32[64,32,512]{2,1,0:T(8,128)} %clear_ref.7, ...), custom_call_target="tpu_custom_call" | custom-call | tf_op jit(solution)/shard_map/pallas_call | solution.py:259
  126.5 0.0 copy-done.3
  126.6 0.0 copy-start.10
  126.6 0.0 copy-start.9
  126.6 0.0 copy-start.5
  126.6 0.0 copy-start.8
  126.6 11.0 %shard_map.178 = (f32[64,32,512]{2,1,0:T(8,128)}, f32[64,32,512]{2,1,0:T(8,128)}, bf16[32,64,512]{2,1,0:T(8,128)(2,1)S(1)}) custom-call(f32[1]{0:T(128)S(6)} %copy.22.rz_ref, f32[8,128]{1,0:T(8,128)S(1)} %get-tuple-element.21.sum_ref, f32[64,32,512]{2,1,0:T(8,128)} %get-tuple-element.22.image_ref, f32[64,32,512]{2,1,0:T(8,128)} %dir_ref.7, ...), custom_call_target="tpu_custom_call" | custom-call | tf_op jit(solution)/shard_map/pallas_call | solution.py:259
  137.7 0.0 copy-start.6
  137.7 1.3 copy-done.6
  139.0 0.0 copy-done.10
  139.0 0.1 dynamic_slice.4
  139.0 0.0 copy-done.9
  139.1 0.2 broadcast_multiply_fusion.refs_2_
  139.3 0.0 copy-done.5
  139.3 0.0 copy-done.8
  139.3 0.0 copy-start.7
  139.3 1.6 copy-done.7
  140.9 95.5 %shard_map.179.h_ref = bf16[32,64,512]{2,1,0:T(8,128)(2,1)S(1)} custom-call(bf16[32,64,512]{2,1,0:T(8,128)(2,1)S(1)} %copy-done.7, bf16[1024,1024]{1,0:T(8,128)(2,1)S(1)} %copy-done.5, f32[2,1024,1]{2,1,0:T(8,128)S(1)} %broadcast_multiply_fusion.refs_2_, f32[1,512]{1,0:T(1,128)S(1)} %bitcast.10, f32[1,1]{1,0:T(1,128)} %bitcast.8.refs_4_), custom_call_target="tpu_custom_call" | custom-call | flops 4294967296 | bytes 4194304 | tf_op jit(solution)/shard_map/pallas_call | solution.py:403
  236.4 12.7 %shard_map.180 = (f32[64,32,512]{2,1,0:T(8,128)}, f32[8,128]{1,0:T(8,128)S(1)}) custom-call(bf16[32,64,512]{2,1,0:T(8,128)(2,1)S(1)} %shard_map.179.h_ref, f32[64,32,512]{2,1,0:T(8,128)} %get-tuple-element.14.res_ref, s32[64,512]{1,0:T(8,128)S(1)} %copy-done.2, s32[64,32,512]{2,1,0:T(8,128)} %clear_ref.7, bf16[512,512]{1,0:T(8,128)(2,1)S(1)} %get-tuple-element.27.day_ref, ...), custom_call_target="tpu_custom_call" | custom-call | tf_op jit(solution)/shard_map/pallas_call | solution.py:259
  249.0 0.0 copy-start
  249.0 2.2 copy-done
  251.2 5.0 %shard_map.181 = f32[64,32,512]{2,1,0:T(8,128)} custom-call(f32[1]{0:T(128)S(6)} %copy.22.rz_ref, f32[8,128]{1,0:T(8,128)S(1)} %get-tuple-element.28.sum_ref, f32[64,32,512]{2,1,0:T(8,128)S(1)} %copy-done, f32[64,32,512]{2,1,0:T(8,128)} %dir_ref.7), custom_call_target="tpu_custom_call" | custom-call | tf_op jit(solution)/shard_map/pallas_call | solution.py:259
  256.2 0.6 reduce_sum.9
Async XLA Ops:
  4.2 0.7 copy-start.4
  8.4 0.9 copy-start.1
  14.9 97.9 %copy-start.2 = (s32[64,512]{1,0:T(8,128)S(1)}, s32[64,512]{1,0:T(8,128)}, u32[]{:S(2)}) copy-start(s32[64,512]{1,0:T(8,128)} %land_ref.7) | copy-start | bytes 393220
  112.9 13.7 %copy-start.3 = (bf16[512,512]{1,0:T(8,128)(2,1)S(1)}, bf16[512,512]{1,0:T(8,128)(2,1)}, u32[]{:S(2)}) copy-start(bf16[512,512]{1,0:T(8,128)(2,1)} %lat_ref.3) | copy-start | bytes 1572868
  126.6 12.4 %copy-start.10 = (f32[32]{0:T(128)S(1)}, f32[32]{0:T(128)}, u32[]{:S(2)}) copy-start(f32[32]{0:T(128)} %param.27) | copy-start | bytes 388
  126.6 12.5 %copy-start.9 = (f32[1024]{0:T(1024)S(1)}, f32[1024]{0:T(1024)}, u32[]{:S(2)}) copy-start(f32[1024]{0:T(1024)} %param.25) | copy-start | bytes 12292
  126.6 12.7 %copy-start.5 = (bf16[1024,1024]{1,0:T(8,128)(2,1)S(1)}, bf16[1024,1024]{1,0:T(8,128)(2,1)}, u32[]{:S(2)}) copy-start(bf16[1024,1024]{1,0:T(8,128)(2,1)} %refs_1_.1) | copy-start | bytes 6291460
  126.6 12.7 %copy-start.8 = (f32[512]{0:T(512)S(1)}, f32[512]{0:T(512)}, u32[]{:S(2)}) copy-start(f32[512]{0:T(512)} %param.26) | copy-start | bytes 6148
  137.7 1.3 copy-start.6
  139.3 1.6 copy-start.7
  249.0 2.2 copy-start
